TPU v7x, 32 devices: a whole 2x2x4 slice. The times are simulated.
32 devices in a mesh: groups: 2 (over y), tensor: 2 (over x), expert: 4 (over z), dp: 2 (over core).
Axes of the slice: x: 2, y: 2, z: 4, core: 2. Of those that a mesh axis runs over, the one named last changes fastest.
Arguments:
- tokens: bfloat16 [32, 6144], P(('groups', 'tensor', 'expert', 'dp')), parts along dimension 0, may hold values from -6 to 6
- routes: int32 [32, 2], P(('groups', 'tensor', 'expert', 'dp')), parts along dimension 0, may hold values from 0 to 3, all different within a row; in each aligned block of 1 rows (0 to 0, 1 to 1, ...) no two rows name the same one
- gates: float32 [32, 2], P(('groups', 'tensor', 'expert', 'dp')), parts along dimension 0, may hold values from 0.1 to 0.9
- w_gate: bfloat16 [4, 6144, 8192], P('expert', 'dp', 'tensor'), may hold values from -0.078125 to 0.078125
- w_up: bfloat16 [4, 6144, 8192], P('expert', 'dp', 'tensor'), may hold values from -0.078125 to 0.078125
- w_down: bfloat16 [4, 8192, 6144], P('expert', 'tensor', 'dp'), may hold values from -0.0625 to 0.0625
Outputs:
- mixed: bfloat16 [32, 6144], P(('groups', 'tensor', 'expert', 'dp')), parts along dimension 0
There are 2 independent parts, one for each index of `groups`. A program takes and returns all parts, laid end to end along the dimension named above; an argument that names none is the same for every part. Nothing has to cross between parts.
Inputs may be any that keep to these rules, and one draw needn't show every extreme that they name: `routes`: each row names two different experts, and every expert is named by some row.
All inputs are finite; a program needn't handle non-finite values.
Results may differ from a plain program's by a relative error of at most 0.009.
Values may be sent and summed in bfloat16 or wider, within the bound.
A program may use at most 448 MiB of HBM per device.

v0:
```python
import functools

import jax
import jax.numpy as jnp
from jax import lax
from jax.experimental import pallas as pl
from jax.experimental.pallas import tpu as pltpu
from jax.sharding import PartitionSpec as P

AXES = ("groups", "tensor", "expert", "dp")
SUB = 8


def remote(src, dst, send_sem, recv_sem, where):
    return pltpu.make_async_remote_copy(
        src_ref=src,
        dst_ref=dst,
        send_sem=send_sem,
        recv_sem=recv_sem,
        device_id=where,
        device_id_type=pl.DeviceIdType.MESH,
    )


def kernel(
    sizes, tok_ref, routes_ref, gates_ref, wg_hbm, wu_hbm, wd_hbm, out_ref,
    wg, wu, wd, tstage, tsend, tline, tall, tflat, x, pown, psend, precv, hid,
    osend, orecv, zstage, zsend, zrecv,
    w_sem, ts_send, ts_recv, tq_send, tq_recv, p_send, p_recv, o_send, o_recv, z_send, z_recv,
):
    n_groups, n_tensor, n_expert, n_dp = sizes
    n_quad, n_line = n_groups * n_tensor, n_expert * n_dp
    nf, _, cf = wg.shape
    nd, ffh, cd = wd.shape
    lanes = tstage.shape[1]
    g, t = lax.axis_index("groups"), lax.axis_index("tensor")
    e, d = lax.axis_index("expert"), lax.axis_index("dp")
    quad, line = g * n_tensor + t, e * n_dp + d

    def line_peer(k):
        peer = lax.rem(line + k, n_line)
        return peer, {"groups": g, "tensor": t, "expert": peer // n_dp, "dp": lax.rem(peer, n_dp)}

    def quad_peer(k):
        peer = lax.rem(quad + k, n_quad)
        return peer, {"groups": peer // n_tensor, "tensor": lax.rem(peer, n_tensor), "expert": e, "dp": d}

    sibling = {"groups": g, "tensor": t, "expert": e, "dp": 1 - d}

    loads = []
    for j in range(nf):
        cols = pl.ds(pl.multiple_of(g * ffh + j * cf, 128), cf)
        loads.append(pltpu.make_async_copy(wg_hbm.at[0, :, cols], wg.at[j], w_sem.at[0, j]))
        loads.append(pltpu.make_async_copy(wu_hbm.at[0, :, cols], wu.at[j], w_sem.at[1, j]))
    half = pl.ds(pl.multiple_of(g * ffh, 16), ffh)
    for j in range(nd):
        loads.append(pltpu.make_async_copy(wd_hbm.at[0, half, pl.ds(j * cd, cd)], wd.at[j], w_sem.at[2, j]))
    for load in loads:
        load.start()

    barrier = pltpu.get_barrier_semaphore()
    for k in range(1, n_line):
        pl.semaphore_signal(barrier, inc=1, device_id=line_peer(k)[1], device_id_type=pl.DeviceIdType.MESH)
    for k in range(1, n_quad):
        pl.semaphore_signal(barrier, inc=1, device_id=quad_peer(k)[1], device_id_type=pl.DeviceIdType.MESH)

    for k in range(n_dp * SUB):
        tstage[k : k + 1, :] = tok_ref[0:1, k * lanes : (k + 1) * lanes].astype(jnp.float32)
    for h in range(n_dp):
        tsend[h] = tstage[h * SUB : (h + 1) * SUB, :].astype(jnp.bfloat16)
    pl.semaphore_wait(barrier, n_line - 1 + n_quad - 1)

    sends = []
    for k in range(1, n_line):
        peer, where = line_peer(k)
        copy = remote(tsend.at[lax.rem(peer, n_dp)], tline.at[line], ts_send.at[k], ts_recv.at[k], where)
        copy.start()
        sends.append(copy)
    tline[line] = tsend[d]
    for k in range(1, n_line):
        source = lax.rem(line + n_line - k, n_line)
        remote(tsend.at[0], tline.at[source], ts_send.at[k], ts_recv.at[k], sibling).wait_recv()

    for k in range(1, n_quad):
        copy = remote(tline, tall.at[quad], tq_send.at[k], tq_recv.at[k], quad_peer(k)[1])
        copy.start()
        sends.append(copy)
    tall[quad] = tline[...]
    for k in range(1, n_quad):
        source = lax.rem(quad + n_quad - k, n_quad)
        remote(tline, tall.at[source], tq_send.at[k], tq_recv.at[k], sibling).wait_recv()
    pair = 2 * n_line
    for p in range(n_quad // 2):
        for i in range(2):
            for s in range(n_line):
                row = (i * n_line + s) * SUB
                block = tall[2 * p + i, s].astype(jnp.float32)
                for b in range(lanes // 128):
                    tflat[b, row : row + SUB, :] = block[:, b * 128 : (b + 1) * 128]
        for s in range(SUB):
            for b in range(lanes // 128):
                part = tflat[b, pl.ds(s, pair, stride=SUB), :]
                col = s * lanes + b * 128
                x[p * pair : (p + 1) * pair, col : col + 128] = part.astype(jnp.bfloat16)

    def finish(j):
        remote(psend.at[j], precv.at[j], p_send.at[j], p_recv.at[j], sibling).wait_recv()
        gate = pown[j, 0] + precv[j, 0].astype(jnp.float32)
        up = pown[j, 1] + precv[j, 1].astype(jnp.float32)
        hid[:, j * cf : (j + 1) * cf] = (gate / (1.0 + jnp.exp(-gate)) * up).astype(jnp.bfloat16)

    for j in range(nf):
        for i, w in enumerate((wg, wu)):
            loads[2 * j + i].wait()
            part = jnp.dot(x[...], w[j], preferred_element_type=jnp.float32)
            pown[j, i] = part
            psend[j, i] = part.astype(jnp.bfloat16)
        copy = remote(psend.at[j], precv.at[j], p_send.at[j], p_recv.at[j], sibling)
        copy.start()
        sends.append(copy)
        if j > 0:
            finish(j - 1)
    finish(nf - 1)

    for j in range(nd):
        loads[2 * nf + j].wait()
        part = jnp.dot(hid[...], wd[j], preferred_element_type=jnp.float32)
        for q in range(n_quad):
            block = part[q * n_line : (q + 1) * n_line]
            osend[j, q] = jnp.concatenate([block[:, :lanes], block[:, lanes:]], axis=0).astype(jnp.bfloat16)
        for k in range(1, n_quad):
            peer, where = quad_peer(k)
            copy = remote(osend.at[j, peer], orecv.at[j, quad], o_send.at[j, k], o_recv.at[j, k], where)
            copy.start()
            sends.append(copy)

    for j in range(nd):
        total = osend[j, quad].astype(jnp.float32)
        for k in range(1, n_quad):
            source = lax.rem(quad + n_quad - k, n_quad)
            remote(osend.at[j, 0], orecv.at[j, source], o_send.at[j, k], o_recv.at[j, k], sibling).wait_recv()
            total += orecv[j, source].astype(jnp.float32)
        for i in range(2):
            for b in range(lanes // 128):
                part = total[i * n_line : (i + 1) * n_line, b * 128 : (b + 1) * 128]
                zstage[b, pl.ds(2 * j + i, n_line, stride=SUB), :] = part
    for s in range(n_line):
        for b in range(lanes // 128):
            part = zstage[b, s * SUB : (s + 1) * SUB, :]
            zsend[s, :, b * 128 : (b + 1) * 128] = part.astype(jnp.bfloat16)
    for k in range(1, n_line):
        peer, where = line_peer(k)
        copy = remote(zsend.at[peer], zrecv.at[line], z_send.at[k], z_recv.at[k], where)
        copy.start()
        sends.append(copy)
    zrecv[line] = zsend[line]
    for k in range(1, n_line):
        source = lax.rem(line + n_line - k, n_line)
        remote(zsend.at[0], zrecv.at[source], z_send.at[k], z_recv.at[k], sibling).wait_recv()

    for h in range(n_dp):
        total = jnp.zeros((SUB, lanes), jnp.float32)
        for i in range(n_expert):
            weight = jnp.float32(0)
            for c in range(routes_ref.shape[1]):
                weight += jnp.where(routes_ref[0, c] == i, gates_ref[0, c], jnp.float32(0))
            total += weight * zrecv[i * n_dp + h].astype(jnp.float32)
        tstage[h * SUB : (h + 1) * SUB, :] = total
    for k in range(n_dp * SUB):
        out_ref[0:1, k * lanes : (k + 1) * lanes] = tstage[k : k + 1, :].astype(jnp.bfloat16)
    for copy in sends:
        copy.wait_send()


def shards(sizes, tokens, routes, gates, w_gate, w_up, w_down):
    n_groups, n_tensor, n_expert, n_dp = sizes
    n_quad, n_line = n_groups * n_tensor, n_expert * n_dp
    rows = n_quad * n_line
    depth, ffh = w_gate.shape[1], w_gate.shape[2] // n_groups
    cf = min(256, ffh)
    nf = ffh // cf
    lanes = depth // SUB
    cd = 2 * lanes
    nd = depth // cd
    bf16, f32 = jnp.bfloat16, jnp.float32
    dma = pltpu.SemaphoreType.DMA
    return pl.pallas_call(
        functools.partial(kernel, sizes),
        out_shape=jax.ShapeDtypeStruct(tokens.shape, bf16),
        in_specs=[
            pl.BlockSpec(memory_space=pltpu.VMEM),
            pl.BlockSpec(memory_space=pltpu.SMEM),
            pl.BlockSpec(memory_space=pltpu.SMEM),
            pl.BlockSpec(memory_space=pl.ANY),
            pl.BlockSpec(memory_space=pl.ANY),
            pl.BlockSpec(memory_space=pl.ANY),
        ],
        out_specs=pl.BlockSpec(memory_space=pltpu.VMEM),
        scratch_shapes=[
            pltpu.VMEM((nf, depth, cf), bf16),
            pltpu.VMEM((nf, depth, cf), bf16),
            pltpu.VMEM((nd, ffh, cd), bf16),
            pltpu.VMEM((n_dp * SUB, lanes), f32),
            pltpu.VMEM((n_dp, SUB, lanes), bf16),
            pltpu.VMEM((n_line, SUB, lanes), bf16),
            pltpu.VMEM((n_quad, n_line, SUB, lanes), bf16),
            pltpu.VMEM((lanes // 128, 2 * n_line * SUB, 128), f32),
            pltpu.VMEM((rows, depth), bf16),
            pltpu.VMEM((nf, 2, rows, cf), f32),
            pltpu.VMEM((nf, 2, rows, cf), bf16),
            pltpu.VMEM((nf, 2, rows, cf), bf16),
            pltpu.VMEM((rows, ffh), bf16),
            pltpu.VMEM((nd, n_quad, 2 * n_line, lanes), bf16),
            pltpu.VMEM((nd, n_quad, 2 * n_line, lanes), bf16),
            pltpu.VMEM((lanes // 128, n_line * SUB, 128), f32),
            pltpu.VMEM((n_line, SUB, lanes), bf16),
            pltpu.VMEM((n_line, SUB, lanes), bf16),
            dma((3, max(nf, nd))),
            dma((n_line,)),
            dma((n_line,)),
            dma((n_quad,)),
            dma((n_quad,)),
            dma((nf,)),
            dma((nf,)),
            dma((nd, n_quad)),
            dma((nd, n_quad)),
            dma((n_line,)),
            dma((n_line,)),
        ],
        compiler_params=pltpu.CompilerParams(
            collective_id=0, has_side_effects=True, vmem_limit_bytes=56 * 1024 * 1024
        ),
    )(tokens, routes, gates, w_gate, w_up, w_down)


def solution(mesh):
    placed = (
        P(AXES, None),
        P(AXES, None),
        P(AXES, None),
        P("expert", "dp", "tensor"),
        P("expert", "dp", "tensor"),
        P("expert", "tensor", "dp"),
    )
    return jax.shard_map(
        functools.partial(shards, tuple(mesh.shape[axis] for axis in AXES)),
        mesh=mesh,
        in_specs=placed,
        out_specs=P(AXES, None),
        check_vma=False,
    )
```

profile of v0, /device:TPU:0, one launch (start us, length us, event | category | flops | bytes accessed | tf_op | source)
XLA Modules:
  0.0 36.7 jit_solution(15879594071052313027)
XLA Ops:
  0.0 35.3 %shard_map.64 = bf16[1,6144]{1,0:T(2,128)(2,1)} custom-call(bf16[1,6144]{1,0:T(2,128)(2,1)} %tok_ref.1, s32[1,2]{1,0:T(1,128)} %routes_ref.1, f32[1,2]{1,0:T(1,128)} %gates_ref.1, bf16[1,3072,4096]{2,1,0:T(8,128)(2,1)} %wg_hbm.1, bf16[1,3072,4096]{2,1,0:T(8,128)(2,1)} %wu_hbm.1, bf16[1,4096,3072]{2,1,0:T(8,128)(2,1)} %wd_hbm.1), custom_call_target="tpu_custom_call" | custom-call | tf_op jit(solution)/shard_map/pallas_call | solution.py:187
  35.3 1.4 %copy.8 = bf16[1,6144]{1,0:T(2,128)(2,1)} copy(bf16[1,6144]{1,0:T(2,128)(2,1)} %shard_map.64) | data formatting | bytes 24576
where the time goes:
time: 36.9 us; the launch traced here: 36.7 us
  Pallas kernels  35.3 us (96%)
  local copies, waits for them, and re-layouts  1.37 us (4%)
    pallas_call x1, Pallas kernels, shards(): pl.pallas_call(functools.partial(kernel, sizes), out_shape=jax.ShapeDtype...  35.3 us
    unnamed x1, local copies, waits for them, and re-layouts  1.37 us

commit v1 on v0

--- a/solution.py
+++ b/solution.py
@@ -33,17 +33,33 @@
     nf, _, cf = wg.shape
     nd, ffh, cd = wd.shape
     lanes = tstage.shape[1]
+    pieces = cd // lanes
     g, t = lax.axis_index("groups"), lax.axis_index("tensor")
     e, d = lax.axis_index("expert"), lax.axis_index("dp")
     quad, line = g * n_tensor + t, e * n_dp + d
 
+    def ahead(at, n):
+        return [at] + [jnp.where(at + k >= n, at + k - n, at + k) for k in range(1, n)]
+
+    def behind(at, n):
+        return [at] + [jnp.where(at >= k, at - k, at + n - k) for k in range(1, n)]
+
+    to_g, to_t, to_e, to_d = ahead(g, n_groups), ahead(t, n_tensor), ahead(e, n_expert), ahead(d, n_dp)
+    from_g, from_t, from_e, from_d = behind(g, n_groups), behind(t, n_tensor), behind(e, n_expert), behind(d, n_dp)
+
     def line_peer(k):
-        peer = lax.rem(line + k, n_line)
-        return peer, {"groups": g, "tensor": t, "expert": peer // n_dp, "dp": lax.rem(peer, n_dp)}
+        pe, pd = to_e[k // n_dp], to_d[k % n_dp]
+        return pe * n_dp + pd, {"groups": g, "tensor": t, "expert": pe, "dp": pd}
+
+    def line_source(k):
+        return from_e[k // n_dp] * n_dp + from_d[k % n_dp]
 
     def quad_peer(k):
-        peer = lax.rem(quad + k, n_quad)
-        return peer, {"groups": peer // n_tensor, "tensor": lax.rem(peer, n_tensor), "expert": e, "dp": d}
+        pg, pt = to_g[k // n_tensor], to_t[k % n_tensor]
+        return pg * n_tensor + pt, {"groups": pg, "tensor": pt, "expert": e, "dp": d}
+
+    def quad_source(k):
+        return from_g[k // n_tensor] * n_tensor + from_t[k % n_tensor]
 
     sibling = {"groups": g, "tensor": t, "expert": e, "dp": 1 - d}
 
@@ -73,12 +89,12 @@
     sends = []
     for k in range(1, n_line):
         peer, where = line_peer(k)
-        copy = remote(tsend.at[lax.rem(peer, n_dp)], tline.at[line], ts_send.at[k], ts_recv.at[k], where)
+        copy = remote(tsend.at[to_d[k % n_dp]], tline.at[line], ts_send.at[k], ts_recv.at[k], where)
         copy.start()
         sends.append(copy)
     tline[line] = tsend[d]
     for k in range(1, n_line):
-        source = lax.rem(line + n_line - k, n_line)
+        source = line_source(k)
         remote(tsend.at[0], tline.at[source], ts_send.at[k], ts_recv.at[k], sibling).wait_recv()
 
     for k in range(1, n_quad):
@@ -87,7 +103,7 @@
         sends.append(copy)
     tall[quad] = tline[...]
     for k in range(1, n_quad):
-        source = lax.rem(quad + n_quad - k, n_quad)
+        source = quad_source(k)
         remote(tline, tall.at[source], tq_send.at[k], tq_recv.at[k], sibling).wait_recv()
     pair = 2 * n_line
     for p in range(n_quad // 2):
@@ -127,7 +143,9 @@
         part = jnp.dot(hid[...], wd[j], preferred_element_type=jnp.float32)
         for q in range(n_quad):
             block = part[q * n_line : (q + 1) * n_line]
-            osend[j, q] = jnp.concatenate([block[:, :lanes], block[:, lanes:]], axis=0).astype(jnp.bfloat16)
+            osend[j, q] = jnp.concatenate(
+                [block[:, i * lanes : (i + 1) * lanes] for i in range(pieces)], axis=0
+            ).astype(jnp.bfloat16)
         for k in range(1, n_quad):
             peer, where = quad_peer(k)
             copy = remote(osend.at[j, peer], orecv.at[j, quad], o_send.at[j, k], o_recv.at[j, k], where)
@@ -137,13 +155,13 @@
     for j in range(nd):
         total = osend[j, quad].astype(jnp.float32)
         for k in range(1, n_quad):
-            source = lax.rem(quad + n_quad - k, n_quad)
+            source = quad_source(k)
             remote(osend.at[j, 0], orecv.at[j, source], o_send.at[j, k], o_recv.at[j, k], sibling).wait_recv()
             total += orecv[j, source].astype(jnp.float32)
-        for i in range(2):
+        for i in range(pieces):
             for b in range(lanes // 128):
                 part = total[i * n_line : (i + 1) * n_line, b * 128 : (b + 1) * 128]
-                zstage[b, pl.ds(2 * j + i, n_line, stride=SUB), :] = part
+                zstage[b, pl.ds(pieces * j + i, n_line, stride=SUB), :] = part
     for s in range(n_line):
         for b in range(lanes // 128):
             part = zstage[b, s * SUB : (s + 1) * SUB, :]
@@ -155,7 +173,7 @@
         sends.append(copy)
     zrecv[line] = zsend[line]
     for k in range(1, n_line):
-        source = lax.rem(line + n_line - k, n_line)
+        source = line_source(k)
         remote(zsend.at[0], zrecv.at[source], z_send.at[k], z_recv.at[k], sibling).wait_recv()
 
     for h in range(n_dp):
@@ -177,10 +195,10 @@
     n_quad, n_line = n_groups * n_tensor, n_expert * n_dp
     rows = n_quad * n_line
     depth, ffh = w_gate.shape[1], w_gate.shape[2] // n_groups
-    cf = min(256, ffh)
+    cf = min(1024, ffh)
     nf = ffh // cf
     lanes = depth // SUB
-    cd = 2 * lanes
+    cd = 4 * lanes
     nd = depth // cd
     bf16, f32 = jnp.bfloat16, jnp.float32
     dma = pltpu.SemaphoreType.DMA
@@ -210,8 +228,8 @@
             pltpu.VMEM((nf, 2, rows, cf), bf16),
             pltpu.VMEM((nf, 2, rows, cf), bf16),
             pltpu.VMEM((rows, ffh), bf16),
-            pltpu.VMEM((nd, n_quad, 2 * n_line, lanes), bf16),
-            pltpu.VMEM((nd, n_quad, 2 * n_line, lanes), bf16),
+            pltpu.VMEM((nd, n_quad, cd // lanes * n_line, lanes), bf16),
+            pltpu.VMEM((nd, n_quad, cd // lanes * n_line, lanes), bf16),
             pltpu.VMEM((lanes // 128, n_line * SUB, 128), f32),
             pltpu.VMEM((n_line, SUB, lanes), bf16),
             pltpu.VMEM((n_line, SUB, lanes), bf16),

time: 36.9 us -> 32.1 us (0.87)
  Pallas kernels: 35.3 us -> 30.5 us
    pallas_call x1, Pallas kernels: 35.3 us -> 30.5 us  [shards(): pl.pallas_call(functools.partial(kernel, sizes), out_shape=jax.ShapeDtype...]
where the time goes in v1:
time: 32.1 us; the launch traced here: 31.9 us
  Pallas kernels  30.5 us (95%)
  local copies, waits for them, and re-layouts  1.37 us (4%)
    pallas_call x1, Pallas kernels, shards(): pl.pallas_call(functools.partial(kernel, sizes), out_shape=jax.ShapeDtype...  30.5 us
    unnamed x1, local copies, waits for them, and re-layouts  1.37 us

profile of v1, /device:TPU:0, one launch (start us, length us, event | category | flops | bytes accessed | tf_op | source)
XLA Modules:
  0.0 31.9 jit_solution(7315890362855334017)
XLA Ops:
  0.0 30.5 %shard_map.64 = bf16[1,6144]{1,0:T(2,128)(2,1)} custom-call(bf16[1,6144]{1,0:T(2,128)(2,1)} %tok_ref.1, s32[1,2]{1,0:T(1,128)} %routes_ref.1, f32[1,2]{1,0:T(1,128)} %gates_ref.1, bf16[1,3072,4096]{2,1,0:T(8,128)(2,1)} %wg_hbm.1, bf16[1,3072,4096]{2,1,0:T(8,128)(2,1)} %wu_hbm.1, bf16[1,4096,3072]{2,1,0:T(8,128)(2,1)} %wd_hbm.1), custom_call_target="tpu_custom_call" | custom-call | tf_op jit(solution)/shard_map/pallas_call | solution.py:205
  30.5 1.4 %copy.8 = bf16[1,6144]{1,0:T(2,128)(2,1)} copy(bf16[1,6144]{1,0:T(2,128)(2,1)} %shard_map.64) | data formatting | bytes 24576
